TPU v7x, 256 devices: a whole 4x4x8 slice. The times are simulated.
256 devices in a mesh: leaf: 256 (over z, y, x, core).
Axes of the slice: x: 4, y: 4, z: 8, core: 2. Of those that a mesh axis runs over, the one named last changes fastest.
Arguments:
- blocks: float32 [65536, 256], P('leaf'), as said below
- generators: float32 [65536, 256], P('leaf'), as said below
- rhs_blocks: float32 [65536, 128], P('leaf'), may hold values from -24 to 24
Outputs:
- solution: float32 [65536, 128], P('leaf')
- logdet_mean: float32 [], replicated
Inputs may be any that keep to these rules, and one draw needn't show every extreme that they name: `blocks`: each block of 256 rows is symmetric positive definite. `generators`: every Schur complement S formed in the merges is symmetric positive definite.
All inputs are finite; a program needn't handle non-finite values.
Results may differ from a plain program's by a relative error of at most 0.0001.
Values sent between devices are 32-bit elements; how exact they have to be, the bound alone decides.
A program may use at most 128 MiB of HBM per device.

v0:
```python
import jax
import jax.numpy as jnp
from jax import lax
from jax.sharding import PartitionSpec as P

HIGHEST = lax.Precision.HIGHEST


def partner(block, axis, stride):
    count = lax.axis_size(axis)
    route = []
    for low in range(count):
        high = low | 1 << stride
        if high != low and high < count:
            route += [(low, high), (high, low)]
    return lax.ppermute(block, axis, route)


def lower_solve(factor, target):
    return jax.scipy.linalg.solve_triangular(factor, target, lower=True)


def upper_solve(factor, target):
    return jax.scipy.linalg.solve_triangular(factor, target, lower=True, trans="T")


def merge_pair(left_block, left_gen, left_rhs, right_block, right_gen, right_rhs):
    coupling = 0.5 * jnp.einsum("ik,jk->ij", left_gen, right_gen, precision=HIGHEST)
    factor = jnp.linalg.cholesky(left_block)
    reduced = lower_solve(factor, coupling)
    carried = lower_solve(factor, left_rhs)
    parent_block = right_block - jnp.einsum("ki,kj->ij", reduced, reduced, precision=HIGHEST)
    parent_rhs = right_rhs - jnp.einsum("ki,kj->ij", reduced, carried, precision=HIGHEST)
    log_det = 2.0 * jnp.sum(jnp.log(jnp.diagonal(factor)))
    return ((parent_block, right_gen, parent_rhs), (factor, reduced, carried), log_det)


def climb(node_state, device_index, first_height, last_height, saved_factors, det_sum):
    for height in range(first_height, last_height + 1):
        own_block, own_gen, own_rhs = node_state
        sibling = partner((own_block, own_gen, own_rhs), "leaf", height - 1)
        side_bit = device_index >> height - 1 & 1
        left_side = side_bit == 0
        left_node = tuple(
            (
                jnp.where(left_side, own_part, peer_part)
                for own_part, peer_part in zip(node_state, sibling)
            )
        )
        right_node = tuple(
            (
                jnp.where(left_side, peer_part, own_part)
                for own_part, peer_part in zip(node_state, sibling)
            )
        )
        node_state, kept, log_det = merge_pair(*left_node, *right_node)
        counted = device_index % 2**height == 0
        det_sum = det_sum + jnp.where(counted, log_det, 0.0)
        saved_factors.append(kept + (side_bit,))
    return (node_state, det_sum)


def local(blocks, generators, rhs_blocks):
    device_index = lax.axis_index("leaf")
    devices = lax.axis_size("leaf")
    height_total = devices.bit_length() - 1
    rank_size = blocks.shape[0]
    saved_factors = []
    det_sum = jnp.zeros((), jnp.float32)
    node_state = (blocks, generators, rhs_blocks)
    node_state, det_sum = climb(node_state, device_index, 1, height_total, saved_factors, det_sum)
    root_block, root_gen, root_rhs = node_state
    root_factor = jnp.linalg.cholesky(root_block)
    det_sum = det_sum + jnp.where(
        device_index == 0, 2.0 * jnp.sum(jnp.log(jnp.diagonal(root_factor))), 0.0
    )
    solution = upper_solve(root_factor, lower_solve(root_factor, root_rhs))
    for factor, reduced, carried, side_bit in reversed(saved_factors):
        target = carried - jnp.einsum("ij,jk->ik", reduced, solution, precision=HIGHEST)
        left_value = upper_solve(factor, target)
        solution = jnp.where(side_bit == 0, left_value, solution)
    det_total = lax.psum(det_sum, "leaf")
    return (solution, det_total / (rank_size * devices))


def solution(mesh):
    in_specs = (P("leaf", None), P("leaf", None), P("leaf", None))
    out_specs = (P("leaf", None), P())
    return jax.shard_map(local, mesh=mesh, in_specs=in_specs, out_specs=out_specs, check_vma=False)
```

profile of v0, /device:TPU:103, one launch (start us, length us, event | category | flops | bytes accessed | tf_op | source)
XLA Modules:
  0.0 852.9 jit_solution(15221312353554256155)
XLA Ops:
  4.8 11.7 %cholesky.424 = f32[128,128]{1,0:T(8,128)S(1)} custom-call(f32[128,128]{1,0:T(8,128)S(1)} %cholesky.726), custom_call_target="Cholesky" | custom-call | tf_op jit(solution)/shard_map/jit(cholesky)/cholesky | solution.py:29
  26.8 11.7 %cholesky.441 = f32[128,128]{1,0:T(8,128)S(1)} custom-call(f32[128,128]{1,0:T(8,128)S(1)} %slice_subtract_fusion.41), custom_call_target="Cholesky" | custom-call | tf_op jit(solution)/shard_map/jit(cholesky)/cholesky | solution.py:29
  44.9 19.7 %custom-call.100 = f32[2,128,128]{1,2,0:T(8,128)S(1)} custom-call(f32[2,128,128]{2,1,0:T(8,128)S(1)} %get-tuple-element.193), custom_call_target="InvertDiagBlocksLowerTriangular" | custom-call | tf_op jit(solution)/shard_map/jit(_solve_triangular)/triangular_solve | solution.py:24
  81.1 11.7 %cholesky.458 = f32[128,128]{1,0:T(8,128)S(1)} custom-call(f32[128,128]{1,0:T(8,128)S(1)} %cholesky.729), custom_call_target="Cholesky" | custom-call | tf_op jit(solution)/shard_map/jit(cholesky)/cholesky | solution.py:29
  103.2 11.7 %cholesky.475 = f32[128,128]{1,0:T(8,128)S(1)} custom-call(f32[128,128]{1,0:T(8,128)S(1)} %slice_subtract_fusion.38), custom_call_target="Cholesky" | custom-call | tf_op jit(solution)/shard_map/jit(cholesky)/cholesky | solution.py:29
  121.6 19.9 %custom-call.99 = f32[2,128,128]{1,2,0:T(8,128)S(1)} custom-call(f32[2,128,128]{2,1,0:T(8,128)S(1)} %get-tuple-element.192), custom_call_target="InvertDiagBlocksLowerTriangular" | custom-call | tf_op jit(solution)/shard_map/jit(_solve_triangular)/triangular_solve | solution.py:24
  159.7 11.7 %cholesky.492 = f32[128,128]{1,0:T(8,128)S(1)} custom-call(f32[128,128]{1,0:T(8,128)S(1)} %cholesky.732), custom_call_target="Cholesky" | custom-call | tf_op jit(solution)/shard_map/jit(cholesky)/cholesky | solution.py:29
  181.7 11.7 %cholesky.509 = f32[128,128]{1,0:T(8,128)S(1)} custom-call(f32[128,128]{1,0:T(8,128)S(1)} %slice_subtract_fusion.35), custom_call_target="Cholesky" | custom-call | tf_op jit(solution)/shard_map/jit(cholesky)/cholesky | solution.py:29
  200.6 19.7 %custom-call.98 = f32[2,128,128]{1,2,0:T(8,128)S(1)} custom-call(f32[2,128,128]{2,1,0:T(8,128)S(1)} %get-tuple-element.191), custom_call_target="InvertDiagBlocksLowerTriangular" | custom-call | tf_op jit(solution)/shard_map/jit(_solve_triangular)/triangular_solve | solution.py:24
  237.5 11.7 %cholesky.526 = f32[128,128]{1,0:T(8,128)S(1)} custom-call(f32[128,128]{1,0:T(8,128)S(1)} %cholesky.735), custom_call_target="Cholesky" | custom-call | tf_op jit(solution)/shard_map/jit(cholesky)/cholesky | solution.py:29
  259.6 11.7 %cholesky.543 = f32[128,128]{1,0:T(8,128)S(1)} custom-call(f32[128,128]{1,0:T(8,128)S(1)} %slice_subtract_fusion.32), custom_call_target="Cholesky" | custom-call | tf_op jit(solution)/shard_map/jit(cholesky)/cholesky | solution.py:29
  278.2 19.7 %custom-call.97 = f32[2,128,128]{1,2,0:T(8,128)S(1)} custom-call(f32[2,128,128]{2,1,0:T(8,128)S(1)} %get-tuple-element.190), custom_call_target="InvertDiagBlocksLowerTriangular" | custom-call | tf_op jit(solution)/shard_map/jit(_solve_triangular)/triangular_solve | solution.py:24
  317.9 11.7 %cholesky.560 = f32[128,128]{1,0:T(8,128)S(1)} custom-call(f32[128,128]{1,0:T(8,128)S(1)} %cholesky.738), custom_call_target="Cholesky" | custom-call | tf_op jit(solution)/shard_map/jit(cholesky)/cholesky | solution.py:29
  340.0 11.7 %cholesky.577 = f32[128,128]{1,0:T(8,128)S(1)} custom-call(f32[128,128]{1,0:T(8,128)S(1)} %slice_subtract_fusion.29), custom_call_target="Cholesky" | custom-call | tf_op jit(solution)/shard_map/jit(cholesky)/cholesky | solution.py:29
  358.8 19.7 %custom-call.96 = f32[2,128,128]{1,2,0:T(8,128)S(1)} custom-call(f32[2,128,128]{2,1,0:T(8,128)S(1)} %get-tuple-element.189), custom_call_target="InvertDiagBlocksLowerTriangular" | custom-call | tf_op jit(solution)/shard_map/jit(_solve_triangular)/triangular_solve | solution.py:24
  395.0 11.7 %cholesky.594 = f32[128,128]{1,0:T(8,128)S(1)} custom-call(f32[128,128]{1,0:T(8,128)S(1)} %cholesky.741), custom_call_target="Cholesky" | custom-call | tf_op jit(solution)/shard_map/jit(cholesky)/cholesky | solution.py:29
  417.0 11.7 %cholesky.611 = f32[128,128]{1,0:T(8,128)S(1)} custom-call(f32[128,128]{1,0:T(8,128)S(1)} %slice_subtract_fusion.26), custom_call_target="Cholesky" | custom-call | tf_op jit(solution)/shard_map/jit(cholesky)/cholesky | solution.py:29
  435.3 19.7 %custom-call.95 = f32[2,128,128]{1,2,0:T(8,128)S(1)} custom-call(f32[2,128,128]{2,1,0:T(8,128)S(1)} %get-tuple-element.188), custom_call_target="InvertDiagBlocksLowerTriangular" | custom-call | tf_op jit(solution)/shard_map/jit(_solve_triangular)/triangular_solve | solution.py:24
  468.0 11.0 %collective-permute-done.19 = f32[256,128]{1,0:T(8,128)} collective-permute-done((f32[256,128]{1,0:T(8,128)}, f32[256,128]{1,0:T(8,128)}, u32[]{:S(2)}, u32[]{:S(2)}) %collective-permute-start.19) | collective-permute-done | bytes 131104 | tf_op jit(solution)/shard_map/ppermute | solution.py:16
  486.1 11.7 %cholesky.628 = f32[128,128]{1,0:T(8,128)S(1)} custom-call(f32[128,128]{1,0:T(8,128)S(1)} %cholesky.744), custom_call_target="Cholesky" | custom-call | tf_op jit(solution)/shard_map/jit(cholesky)/cholesky | solution.py:29
  500.0 11.3 %custom-call.84 = f32[1,128,128]{1,2,0:T(8,128)} custom-call(f32[1,128,128]{2,1,0:T(8,128)} %get-tuple-element.313), custom_call_target="InvertDiagBlocksLowerTriangular" | custom-call | tf_op jit(solution)/shard_map/jit(cholesky)/cholesky | solution.py:29
  513.2 12.5 %cholesky.645 = f32[128,128]{1,0:T(8,128)S(1)} custom-call(f32[128,128]{1,0:T(8,128)} %slice_subtract_fusion.23), custom_call_target="Cholesky" | custom-call | tf_op jit(solution)/shard_map/jit(cholesky)/cholesky | solution.py:29
  538.2 21.1 %custom-call.94 = f32[2,128,128]{1,2,0:T(8,128)} custom-call(f32[2,128,128]{2,1,0:T(8,128)} %get-tuple-element.187), custom_call_target="InvertDiagBlocksLowerTriangular" | custom-call | tf_op jit(solution)/shard_map/jit(_solve_triangular)/triangular_solve | solution.py:24
  587.0 11.7 %cholesky.662 = f32[128,128]{1,0:T(8,128)S(1)} custom-call(f32[128,128]{1,0:T(8,128)S(1)} %cholesky.747), custom_call_target="Cholesky" | custom-call | tf_op jit(solution)/shard_map/jit(cholesky)/cholesky | solution.py:29
  598.7 10.4 %custom-call.87 = f32[1,128,128]{1,2,0:T(8,128)} custom-call(f32[1,128,128]{2,1,0:T(8,128)S(1)} %get-tuple-element.309), custom_call_target="InvertDiagBlocksLowerTriangular" | custom-call | tf_op jit(solution)/shard_map/jit(cholesky)/cholesky | solution.py:29
  611.4 11.7 %cholesky.679 = f32[128,128]{1,0:T(8,128)S(1)} custom-call(f32[128,128]{1,0:T(8,128)S(1)} %slice_subtract_fusion.20), custom_call_target="Cholesky" | custom-call | tf_op jit(solution)/shard_map/jit(cholesky)/cholesky | solution.py:29
  635.4 20.7 %custom-call.93 = f32[2,128,128]{1,2,0:T(8,128)} custom-call(f32[2,128,128]{2,1,0:T(8,128)S(1)} %get-tuple-element.186), custom_call_target="InvertDiagBlocksLowerTriangular" | custom-call | tf_op jit(solution)/shard_map/jit(_solve_triangular)/triangular_solve | solution.py:24
  664.0 11.7 %cholesky.696 = f32[128,128]{1,0:T(8,128)S(1)} custom-call(f32[128,128]{1,0:T(8,128)S(1)} %cholesky.750), custom_call_target="Cholesky" | custom-call | tf_op jit(solution)/shard_map/jit(cholesky)/cholesky | solution.py:73
  677.8 11.3 %custom-call.90 = f32[1,128,128]{1,2,0:T(8,128)} custom-call(f32[1,128,128]{2,1,0:T(8,128)} %get-tuple-element.305), custom_call_target="InvertDiagBlocksLowerTriangular" | custom-call | tf_op jit(solution)/shard_map/jit(cholesky)/cholesky | solution.py:73
  691.9 13.2 %cholesky.713 = f32[128,128]{1,0:T(8,128)} custom-call(f32[128,128]{1,0:T(8,128)} %convolution_subtract_fusion.17), custom_call_target="Cholesky" | custom-call | tf_op jit(solution)/shard_map/jit(cholesky)/cholesky | solution.py:73
  716.8 82.0 %psum.7 = f32[]{:T(128)} all-reduce(f32[]{:T(128)S(6)} %add.108), channel_id=1, replica_groups=mesh['leaf'=256] {'leaf'}, use_global_device_ids=true, to_apply=%region_13.18 | all-reduce | flops 1 | bytes 8 | tf_op jit(solution)/shard_map/psum | solution.py:82
  805.2 20.5 %custom-call.92 = f32[2,128,128]{1,2,0:T(8,128)S(1)} custom-call(f32[2,128,128]{2,1,0:T(8,128)} %copy-done.100), custom_call_target="InvertDiagBlocksLowerTriangular" | custom-call | tf_op jit(solution)/shard_map/jit(_solve_triangular)/triangular_solve | solution.py:24
  (585 shorter events, 350.5 us)
Async XLA Ops:
  1.8 2.7 collective-permute-start
  2.7 61.9 %collective-permute-start.2 = (f32[256,256]{0,1:T(8,128)S(1)}, f32[256,256]{0,1:T(8,128)S(1)}, u32[]{:S(2)}, u32[]{:S(2)}) collective-permute-start(f32[256,256]{0,1:T(8,128)S(1)} %copy.32), channel_id=1, source_target_pairs={{0,1},{1,0},{2,3},{3,2},{4,5},{5,4},{6,7},{7,6},{8,9},{9,8},{10,11... | collective-permute-start | bytes 786440 | tf_op jit(solution)/shard_map/ppermute | solution.py:16
  2.8 1.7 collective-permute-start.1
  64.7 76.8 %collective-permute-start.5 = (f32[256,256]{0,1:T(8,128)S(1)}, f32[256,256]{0,1:T(8,128)S(1)}, u32[]{:S(2)}, u32[]{:S(2)}) collective-permute-start(f32[256,256]{0,1:T(8,128)S(1)} %broadcast_select_fusion.13), channel_id=1, source_target_pairs={{0,2},{2,0},{1,3},{3,1},{4,6},{6,4},{5,7},{7,5},{8,10},{10,8},{9,1... | collective-permute-start | bytes 786440 | tf_op jit(solution)/shard_map/ppermute | solution.py:16
  68.4 6.9 collective-permute-start.4
  69.9 10.9 %collective-permute-start.3 = (f32[256,256]{0,1:T(8,128)S(1)}, f32[256,256]{0,1:T(8,128)S(1)}, u32[]{:S(2)}, u32[]{:S(2)}) collective-permute-start(f32[256,256]{0,1:T(8,128)S(1)} %select_subtract_fusion.7), channel_id=1, source_target_pairs={{0,2},{2,0},{1,3},{3,1},{4,6},{6,4},{5,7},{7,5},{8,10},{10,8},{9,1... | collective-permute-start | bytes 786440 | tf_op jit(solution)/shard_map/ppermute | solution.py:16
  141.5 78.7 %collective-permute-start.8 = (f32[256,256]{0,1:T(8,128)S(1)}, f32[256,256]{0,1:T(8,128)S(1)}, u32[]{:S(2)}, u32[]{:S(2)}) collective-permute-start(f32[256,256]{0,1:T(8,128)S(1)} %broadcast_select_fusion.11), channel_id=1, source_target_pairs={{0,4},{4,0},{1,5},{5,1},{2,6},{6,2},{3,7},{7,3},{8,12},{12,8},{9,1... | collective-permute-start | bytes 786440 | tf_op jit(solution)/shard_map/ppermute | solution.py:16
  145.8 7.6 collective-permute-start.7
  150.7 8.1 collective-permute-start.6
  220.3 4.0 copy-start.22
  220.3 77.6 %collective-permute-start.11 = (f32[256,256]{0,1:T(8,128)S(1)}, f32[256,256]{0,1:T(8,128)S(1)}, u32[]{:S(2)}, u32[]{:S(2)}) collective-permute-start(f32[256,256]{0,1:T(8,128)S(1)} %broadcast_select_fusion.9), channel_id=1, source_target_pairs={{0,8},{8,0},{1,9},{9,1},{2,10},{10,2},{3,11},{11,3},{4,12},{12,4},... | collective-permute-start | bytes 786440 | tf_op jit(solution)/shard_map/ppermute | solution.py:16
  225.9 6.0 collective-permute-start.10
  229.2 7.4 collective-permute-start.9
  297.9 5.1 copy-start.24
  298.0 80.5 %collective-permute-start.14 = (f32[256,256]{0,1:T(8,128)S(1)}, f32[256,256]{0,1:T(8,128)}, u32[]{:S(2)}, u32[]{:S(2)}) collective-permute-start(f32[256,256]{0,1:T(8,128)S(1)} %broadcast_select_fusion.7), channel_id=1, source_target_pairs={{0,16},{16,0},{1,17},{17,1},{2,18},{18,2},{3,19},{19,3},{4,20},{20... | collective-permute-start | bytes 786440 | tf_op jit(solution)/shard_map/ppermute | solution.py:16
  304.5 7.6 collective-permute-start.13
  308.2 8.8 %collective-permute-start.12 = (f32[256,256]{0,1:T(8,128)S(1)}, f32[256,256]{0,1:T(8,128)S(1)}, u32[]{:S(2)}, u32[]{:S(2)}) collective-permute-start(f32[256,256]{0,1:T(8,128)S(1)} %select_subtract_fusion.4), channel_id=1, source_target_pairs={{0,16},{16,0},{1,17},{17,1},{2,18},{18,2},{3,19},{19,3},{4,20},{20... | collective-permute-start | bytes 786440 | tf_op jit(solution)/shard_map/ppermute | solution.py:16
  379.5 75.5 %collective-permute-start.17 = (f32[256,256]{0,1:T(8,128)S(1)}, f32[256,256]{0,1:T(8,128)}, u32[]{:S(2)}, u32[]{:S(2)}) collective-permute-start(f32[256,256]{0,1:T(8,128)S(1)} %broadcast_select_fusion.5), channel_id=1, source_target_pairs={{0,32},{32,0},{1,33},{33,1},{2,34},{34,2},{3,35},{35,3},{4,36},{36... | collective-permute-start | bytes 786440 | tf_op jit(solution)/shard_map/ppermute | solution.py:16
  383.8 6.3 copy-start.35
  383.8 6.3 collective-permute-start.16
  388.3 5.7 collective-permute-start.15
  455.1 104.3 %collective-permute-start.20 = (f32[256,256]{0,1:T(8,128)S(1)}, f32[256,256]{0,1:T(8,128)}, u32[]{:S(2)}, u32[]{:S(2)}) collective-permute-start(f32[256,256]{0,1:T(8,128)S(1)} %broadcast_select_fusion.3), channel_id=1, source_target_pairs={{0,64},{64,0},{1,65},{65,1},{2,66},{66,2},{3,67},{67,3},{4,68},{68... | collective-permute-start | bytes 786440 | tf_op jit(solution)/shard_map/ppermute | solution.py:16
  458.2 5.1 copy-start.5
  461.0 18.0 %collective-permute-start.19 = (f32[256,128]{1,0:T(8,128)}, f32[256,128]{1,0:T(8,128)}, u32[]{:S(2)}, u32[]{:S(2)}) collective-permute-start(f32[256,128]{1,0:T(8,128)} %select_subtract_fusion.10), channel_id=1, source_target_pairs={{0,64},{64,0},{1,65},{65,1},{2,66},{66,2},{3,67},{67,3},{4,68},{68... | collective-permute-start | bytes 393224 | tf_op jit(solution)/shard_map/ppermute | solution.py:16
  466.3 18.2 %collective-permute-start.18 = (f32[256,256]{0,1:T(8,128)S(1)}, f32[256,256]{0,1:T(8,128)S(1)}, u32[]{:S(2)}, u32[]{:S(2)}) collective-permute-start(f32[256,256]{0,1:T(8,128)S(1)} %select_subtract_fusion.2), channel_id=1, source_target_pairs={{0,64},{64,0},{1,65},{65,1},{2,66},{66,2},{3,67},{67,3},{4,68},{68... | collective-permute-start | bytes 786440 | tf_op jit(solution)/shard_map/ppermute | solution.py:16
  466.7 18.5 %copy-start.2 = (f32[256,256]{0,1:T(8,128)S(1)}, f32[256,256]{0,1:T(8,128)}, u32[]{:S(2)}) copy-start(f32[256,256]{0,1:T(8,128)} %copy-done.1) | copy-start | bytes 786436
  486.1 25.1 %copy-start.65 = (f32[256,256]{1,0:T(8,128)S(1)}, f32[256,256]{1,0:T(8,128)}, u32[]{:S(2)}) copy-start(f32[256,256]{1,0:T(8,128)} %copy-done.64) | copy-start | bytes 786436
  559.4 7.6 copy-start.30
  559.4 96.7 %collective-permute-start.23 = (f32[256,256]{0,1:T(8,128)S(1)}, f32[256,256]{0,1:T(8,128)}, u32[]{:S(2)}, u32[]{:S(2)}) collective-permute-start(f32[256,256]{0,1:T(8,128)S(1)} %broadcast_select_fusion.1), channel_id=1, source_target_pairs={{0,128},{128,0},{1,129},{129,1},{2,130},{130,2},{3,131},{131,3},{4... | collective-permute-start | bytes 786440 | tf_op jit(solution)/shard_map/ppermute | solution.py:16
  569.8 13.6 %collective-permute-start.21 = (f32[256,256]{0,1:T(8,128)}, f32[256,256]{0,1:T(8,128)}, u32[]{:S(2)}, u32[]{:S(2)}) collective-permute-start(f32[256,256]{0,1:T(8,128)} %select_subtract_fusion.1), channel_id=1, source_target_pairs={{0,128},{128,0},{1,129},{129,1},{2,130},{130,2},{3,131},{131,3},{4... | collective-permute-start | bytes 786440 | tf_op jit(solution)/shard_map/ppermute | solution.py:16
  574.1 141.1 %collective-permute-start.22 = (f32[256,128]{1,0:T(8,128)}, f32[256,128]{1,0:T(8,128)}, u32[]{:S(2)}, u32[]{:S(2)}) collective-permute-start(f32[256,128]{1,0:T(8,128)} %select_subtract_fusion.9), channel_id=1, source_target_pairs={{0,128},{128,0},{1,129},{129,1},{2,130},{130,2},{3,131},{131,3},{4... | collective-permute-start | bytes 393224 | tf_op jit(solution)/shard_map/ppermute | solution.py:16
  798.9 26.9 %copy-start.33 = (f32[2,128,128]{1,2,0:T(8,128)S(1)}, f32[2,128,128]{1,2,0:T(8,128)}, u32[]{:S(2)}) copy-start(f32[2,128,128]{1,2,0:T(8,128)} %custom-call.93) | copy-start | bytes 393220
  (93 other events, 115.5 us)
where the time goes:
time: 870 us; the launch traced here: 853 us
  other arithmetic  521 us (60%)
  local copies, waits for them, and re-layouts  93 us (11%)
  blocking collectives  82 us (9%)
  matrix products  55.9 us (6%)
  waiting for transfers between devices  42.3 us (5%)
  starting transfers between devices  33.6 us (4%)
  between operations  22.5 us (3%)
    another operation x55, other arithmetic, merge_pair(): factor = jnp.linalg.cholesky(left_block)  280 us
    another operation x19, other arithmetic, upper_solve(): jax.scipy.linalg.solve_triangular(factor, target, lower=True, trans='T')  185 us
    psum x1, blocking collectives, local(): det_total = lax.psum(det_sum, 'leaf')  82 us
    ppermute x24, waiting for transfers between devices, partner(): return lax.ppermute(block, axis, route)  42.3 us
    another operation x64, local copies, waits for them, and re-layouts, upper_solve(): jax.scipy.linalg.solve_triangular(factor, target, lower=True, trans='T')  40.5 us
    another operation x7, other arithmetic, local(): root_factor = jnp.linalg.cholesky(root_block)  39.1 us
    ppermute x24, starting transfers between devices, partner(): return lax.ppermute(block, axis, route)  33.6 us
    unnamed x204, local copies, waits for them, and re-layouts  26.8 us
  transfers between devices with their start and end apart: 24, of which 10 were waited for; matrix products, arithmetic and copies ran while one was open for 70% of the time, Pallas kernels for 0%

commit v1 on v0

v1 whole, which is shorter than its diff:
```python
import functools

import jax
import jax.numpy as jnp
from jax import lax
from jax.experimental import pallas as pl
from jax.experimental.pallas import tpu as pltpu
from jax.sharding import PartitionSpec as P

F32 = jnp.float32
B16 = jnp.bfloat16
MESH = pl.DeviceIdType.MESH
G = 8
B = 64

def iota(shape, dim): return lax.broadcasted_iota(jnp.int32, shape, dim)

def group(tiles, pt, j, l, G, zero, put):
    b = tiles[0].shape[0]
    T = tiles[pt]
    call = [jnp.broadcast_to(T[j:, l+t:l+t+1], (b-j, 128)) for t in range(G)]
    c = [x[:G] + zero for x in call]
    D = [X[j:j+G] for X in tiles]
    lane = iota((8, 128), 1); sub = iota((G, 128), 0)
    for q in range(0, G, 4):
        p = lambda s, t: jnp.broadcast_to(c[q+t][q+s:q+s+1], (8, 128))
        a, bb, d = p(0,0), p(0,1), p(1,1)
        e, f, g, h = p(0,2), p(0,3), p(1,2), p(1,3)
        m, n, o = p(2,2), p(2,3), p(3,3)
        det1 = a*d - bb*bb
        i1 = 1.0/det1
        t00, t01 = d*e - bb*g, d*f - bb*h
        t10, t11 = a*g - bb*e, a*h - bb*f
        m2 = m - i1*(e*t00 + g*t10)
        n2 = n - i1*(e*t01 + g*t11)
        o2 = o - i1*(f*t01 + h*t11)
        det2 = m2*o2 - n2*n2
        i2 = 1.0/det2
        u00, u01, u10, u11 = i1*t00, i1*t01, i1*t10, i1*t11
        ia, ib, id_ = i1*a, i1*bb, i1*d
        ja, jb, jd = i2*m2, i2*n2, i2*o2
        put(None, j+q, (det1, det2))
        def apply(X, piv):
            r = [jnp.broadcast_to(X[q+t:q+t+1], (8, 128)) for t in range(4)]
            if piv:
                inp = (lane >= l+q) & (lane < l+q+4)
                r = [jnp.where(inp, jnp.where(lane == l+q+t, 1.0, 0.0), r[t]) for t in range(4)]
            y0, y1 = id_*r[0] - ib*r[1], ia*r[1] - ib*r[0]
            z2 = r[2] - (e*y0 + g*y1)
            z3 = r[3] - (f*y0 + h*y1)
            w2 = jd*z2 - jb*z3
            w3 = ja*z3 - jb*z2
            w0 = (y0 - u01*w3) - u00*w2
            w1 = (y1 - u11*w3) - u10*w2
            W = [w0, w1, w2, w3]
            out = []
            for v in range(G//8):
                xv = X[8*v:8*v+8]
                if piv: xv = jnp.where(inp, 0.0, xv)
                cv = [c[q+t][8*v:8*v+8] for t in range(4)]
                nv = (xv - (cv[2]*w2 + cv[3]*w3)) - (cv[0]*w0 + cv[1]*w1)
                if q//8 == v:
                    for t in range(4): nv = jnp.where(sub[:8] == q%8+t, W[t], nv)
                out.append(nv)
            return jnp.concatenate(out, 0) if len(out) > 1 else out[0]
        nc = list(c)
        for t in range(q+4, G): nc[t] = apply(c[t], False)
        D = [apply(D[i], i == pt) for i in range(len(tiles))]
        c = nc
    out = []
    inpG = (lane >= l) & (lane < l+G)
    for ti, X in enumerate(tiles):
        put(ti, j, D[ti])
        vs = [X[:j+G]]
        if j+G < b:
            R = [jnp.broadcast_to(D[ti][t:t+1], (8, 128)) for t in range(G)]
            for v in range(G//8, (b-j)//8):
                xv = X[j+8*v:j+8*v+8]
                if ti == pt: xv = jnp.where(inpG, 0.0, xv)
                acc = [None]*4
                for t in range(G):
                    pr = call[t][8*v:8*v+8]*R[t]
                    k = t % 4
                    acc[k] = pr if acc[k] is None else acc[k] + pr
                vs.append(xv - ((acc[0]+acc[1]) + (acc[2]+acc[3])))
        out.append(jnp.concatenate(vs, 0) if len(vs) > 1 else vs[0])
    return out

def split(x):
    hi = x.astype(B16); return hi, (x - hi.astype(F32)).astype(B16)
def mm3(a, b, dn):
    (ah, al), (bh, bl) = a, b
    dg = lambda u, v: lax.dot_general(u, v, dn, preferred_element_type=F32)
    return dg(ah, bh) + (dg(ah, bl) + dg(al, bh))
NN = (((1,), (0,)), ((), ()))
TN = (((0,), (0,)), ((), ()))
NT = (((1,), (1,)), ((), ()))


def copy_to(src, dst, send, recv, device):
    return pltpu.make_async_remote_copy(
        src_ref=src, dst_ref=dst, send_sem=send, recv_sem=recv, device_id=(device,), device_id_type=MESH
    )


def kernel(n, s_in, w_in, g_in, x_out, ld_out, S, W, Wp, Up, up, Uo, uo, CG, Rs, ZC, RC, E, Y, Yp, det, zero_ref,
           sw, rw, sU, rU, su, ru, sx, rx):
    height = n.bit_length() - 1
    me = lax.axis_index("leaf")
    k1 = me + 1
    has = [k1 % (2 << l) == 0 for l in range(height)]
    child = [me - (1 << l) for l in range(height)]
    depth = sum(h.astype(jnp.int32) for h in has)
    parent = me + 1 + sum(jnp.where(has[l], 1 << l, 0) for l in range(height))
    inner = me != n - 1
    R, M = g_in.shape
    nk = R // B

    barrier = pltpu.get_barrier_semaphore()
    for l in range(height):
        @pl.when(has[l])
        def _():
            pl.semaphore_signal(barrier, inc=1, device_id=(child[l],), device_id_type=MESH)
    @pl.when(inner)
    def _():
        pl.semaphore_signal(barrier, inc=1, device_id=(parent,), device_id_type=MESH)
    pl.semaphore_wait(barrier, depth + inner.astype(jnp.int32))

    s0 = s_in[...]
    eye = iota((R, R), 0) == iota((R, R), 1)
    diag = jnp.where(eye, s0, 0.0)
    drow = jnp.sum(diag, axis=0, keepdims=True)
    scol = lax.rsqrt(jnp.sum(diag, axis=1, keepdims=True))
    W[...] = w_in[...] * scol
    for l in range(height):
        @pl.when(has[l])
        def _():
            copy_to(W, Wp, sw.at[l], rw, child[l]).start()
    S[...] = s0 * scol * lax.rsqrt(drow)
    CG[:, R:] = g_in[...] * scol
    zero_ref[...] = jnp.zeros_like(zero_ref)
    own = jnp.sum(jnp.log(drow), axis=1, keepdims=True)

    @pl.when(inner)
    def _():
        copy_to(W, Wp, sw.at[0], rw, parent).wait_recv()
        CG[:, :R] = 0.5 * mm3(split(W[...]), split(Wp[...]), NT)
    @pl.when(jnp.logical_not(inner))
    def _():
        CG[:, :R] = jnp.zeros((R, R), F32)

    for l in range(height):
        @pl.when(has[l])
        def _():
            copy_to(Uo, Up.at[l], sU, rU.at[l], parent).wait_recv()
            S[...] += Up[l]
            copy_to(uo, up.at[l], su, ru.at[l], parent).wait_recv()
            CG[:, R:] += up[l, :R]

    zero = zero_ref[...]
    row = iota((B, 128), 0)
    lane = iota((B, 128), 1)
    for k in range(nk):
        pt, lb = (B * k) // 128, (B * k) % 128
        rows = slice(B * k, B * k + B)
        t0 = pt
        tiles = [S[rows, 128 * t:128 * t + 128] for t in range(t0, R // 128)]
        def put(ti, j, val):
            if ti is None:
                r0 = (B * k + j) // 2
                det[r0:r0 + 1, :] = val[0][0:1]
                det[r0 + 1:r0 + 2, :] = val[1][0:1]
            else:
                Rs[B * k + j:B * k + j + G, 128 * (t0 + ti):128 * (t0 + ti) + 128] = val
        for j in range(0, B, G):
            tiles = group(tiles, 0, j, lb + j, G, zero, put)
        Z = jnp.concatenate(tiles, 1) if len(tiles) > 1 else tiles[0]
        S[rows, 128 * t0:] = Z
        lo = B * (k + 1)
        zs = split(Z)
        if k < nk - 1:
            upd = mm3(zs, split(Rs[rows, 128 * t0:]), TN)
            S[lo:, 128 * t0:] -= upd[lo - 128 * t0:]
        rel = lane - lb
        inside = (rel >= 0) & (rel < B)
        Lk = jnp.where(inside & (rel < G * (row // G)), tiles[0], jnp.where(rel == row, 1.0, 0.0))
        DLk = jnp.where(inside & (rel < G * (row // G) + G), Rs[rows, 128 * t0:128 * t0 + 128], 0.0)
        S[rows, 128 * t0:128 * t0 + 128] = Lk
        both = mm3(split(jnp.concatenate([Lk, DLk], 0)), split(CG[128 * pt:128 * pt + 128, :]), NN)
        ZC[rows, :] = both[:B, :R]
        RC[rows, :] = both[B:]
        if k < nk - 1:
            upd = mm3(zs, split(RC[rows, :]), TN)
            CG[lo:, :] -= upd[lo - 128 * t0:]
        if k == nk - 2:
            upd = mm3(split(ZC[:lo, :]), split(RC[:lo, :]), TN)
            Uo[...] = -upd[:, :R]
            uo[:R, :] = -upd[:, R:]
    rows = slice(R - B, R)
    upd = mm3(split(ZC[rows, :]), split(RC[rows, :]), TN)
    Uo[...] -= upd[:, :R]
    @pl.when(inner)
    def _():
        for l in range(height):
            @pl.when(depth == l)
            def _():
                copy_to(Uo, Up.at[l], sU, rU.at[l], parent).start()
    uo[:R, :] -= upd[:, R:]
    own = own + jnp.sum(jnp.log(det[...]), axis=0, keepdims=True)
    ld_out[...] = jnp.broadcast_to(own, (8, 128))
    for l in range(height):
        @pl.when(has[l])
        def _():
            ld_out[...] += up[l, R:]
    uo[R:, :] = ld_out[...]
    @pl.when(inner)
    def _():
        for l in range(height):
            @pl.when(depth == l)
            def _():
                copy_to(uo, up.at[l], su, ru.at[l], parent).start()

    for k in reversed(range(nk)):
        pt = (B * k) // 128
        rows = slice(B * k, B * k + B)
        hi = B * (k + 1)
        rhs = RC[rows, :]
        if k < nk - 1:
            base = 128 * pt
            r = Rs[rows, base:]
            r = jnp.where(iota(r.shape, 1) >= hi - base, r, 0.0)
            e = E[base:, :]
            e = jnp.where(iota(e.shape, 0) >= hi - base, e, 0.0)
            rhs = rhs - mm3(split(r), split(e), NN)
        sol = mm3(split(S[rows, 128 * pt:128 * pt + 128]), split(rhs), TN)
        E[rows, :] = sol[B * k - 128 * pt:B * k - 128 * pt + B]

    @pl.when(inner)
    def _():
        copy_to(Y, Yp, sx.at[0], rx, parent).wait_recv()
        Y[:R, :] = E[:, R:] - mm3(split(E[:, :R]), split(Yp[:R, :]), NN)
        Y[R:, :] = Yp[R:, :]
    @pl.when(jnp.logical_not(inner))
    def _():
        Y[:R, :] = E[:, R:]
        Y[R:, :] = ld_out[...] / (R * n)
    for l in reversed(range(height)):
        @pl.when(has[l])
        def _():
            copy_to(Y, Yp, sx.at[l], rx, child[l]).start()
    x_out[...] = Y[:R, :] * scol
    ld_out[...] = Y[R:, :]
    for l in range(height):
        @pl.when(has[l])
        def _():
            copy_to(W, Wp, sw.at[l], rw, child[l]).wait_send()
            copy_to(Y, Yp, sx.at[l], rx, child[l]).wait_send()
    @pl.when(inner)
    def _():
        copy_to(Uo, Up.at[0], sU, rU.at[0], parent).wait_send()
        copy_to(uo, up.at[0], su, ru.at[0], parent).wait_send()


def local(n, blocks, generators, rhs_blocks):
    R, M = rhs_blocks.shape
    height = n.bit_length() - 1
    dma = pltpu.SemaphoreType.DMA
    vm = lambda *s: pltpu.VMEM(s, F32)
    x, ld = pl.pallas_call(
        functools.partial(kernel, n),
        out_shape=(jax.ShapeDtypeStruct((R, M), F32), jax.ShapeDtypeStruct((8, 128), F32)),
        in_specs=[pl.BlockSpec(memory_space=pltpu.VMEM)] * 3,
        out_specs=[pl.BlockSpec(memory_space=pltpu.VMEM)] * 2,
        scratch_shapes=[
            vm(R, R), vm(R, R), vm(R, R), vm(height, R, R), vm(height, R + 8, M), vm(R, R), vm(R + 8, M),
            vm(R, R + M), vm(R, R), vm(R, R), vm(R, R + M), vm(R, R + M), vm(R + 8, M), vm(R + 8, M), vm(R // 2, 128), vm(G, 128),
            dma((height,)), dma, dma, dma((height,)), dma, dma((height,)), dma((height,)), dma,
        ],
        compiler_params=pltpu.CompilerParams(
            collective_id=0, has_side_effects=True, vmem_limit_bytes=40 * 1024 * 1024
        ),
        name="ulv",
    )(blocks, generators, rhs_blocks)
    return x, ld[0, 0]


def solution(mesh):
    n = mesh.shape["leaf"]
    return jax.shard_map(
        functools.partial(local, n),
        mesh=mesh,
        in_specs=(P("leaf", None), P("leaf", None), P("leaf", None)),
        out_specs=(P("leaf", None), P()),
        check_vma=False,
    )
```

time: 870 us -> 161 us (0.19)
  the two profiles are of different devices: /device:TPU:103 before, /device:TPU:1 now
where the time goes in v1:
time: 161 us
  Pallas kernels  156 us (97%)
  local copies, waits for them, and re-layouts  3.96 us (2%)
    pallas_call x1, Pallas kernels, local(): pl.pallas_call(functools.partial(kernel, n), out_shape=(jax.ShapeDtypeStr...  156 us
    unnamed x7, local copies, waits for them, and re-layouts  3.45 us

profile of v1, /device:TPU:1, one launch (start us, length us, event | category | flops | bytes accessed | tf_op | source)
XLA Modules:
  0.0 160.6 jit_solution(18027300985965050289)
XLA Ops:
  0.6 0.0 copy-start
  0.6 0.9 copy-done
  1.6 0.0 copy-start.1
  1.6 0.9 copy-done.1
  2.5 0.0 copy-start.2
  2.5 0.9 copy-done.2
  3.4 156.0 %ulv.1 = (f32[256,128]{1,0:T(8,128)S(1)}, f32[8,128]{1,0:T(8,128)S(1)}) custom-call(f32[256,256]{1,0:T(8,128)S(1)} %copy-done, f32[256,256]{1,0:T(8,128)S(1)} %copy-done.1, f32[256,128]{1,0:T(8,128)S(1)} %copy-done.2), custom_call_target="tpu_custom_call" | custom-call | tf_op jit(solution)/shard_map/ulv/pallas_call | solution.py:269
  159.5 0.5 slice.3
  160.0 0.7 copy.6
Async XLA Ops:
  0.6 1.0 copy-start
  1.6 0.9 copy-start.1
  2.5 0.9 copy-start.2

commit v2 on v1

v2 whole, which is shorter than its diff:
```python
import functools

import jax
import jax.numpy as jnp
from jax import lax
from jax.experimental import pallas as pl
from jax.experimental.pallas import tpu as pltpu
from jax.sharding import PartitionSpec as P

F32 = jnp.float32
B16 = jnp.bfloat16
MESH = pl.DeviceIdType.MESH
G = 8
B = 64
NC = 2

def iota(shape, dim): return lax.broadcasted_iota(jnp.int32, shape, dim)

def group(tiles, pt, j, l, G, zero, put):
    b = tiles[0].shape[0]
    T = tiles[pt]
    call = [jnp.broadcast_to(T[j:, l+t:l+t+1], (b-j, 128)) for t in range(G)]
    c = [x[:G] + zero for x in call]
    D = [X[j:j+G] for X in tiles]
    lane = iota((8, 128), 1); sub = iota((G, 128), 0)
    for q in range(0, G, 4):
        p = lambda s, t: jnp.broadcast_to(c[q+t][q+s:q+s+1], (8, 128))
        a, bb, d = p(0,0), p(0,1), p(1,1)
        e, f, g, h = p(0,2), p(0,3), p(1,2), p(1,3)
        m, n, o = p(2,2), p(2,3), p(3,3)
        det1 = a*d - bb*bb
        i1 = 1.0/det1
        t00, t01 = d*e - bb*g, d*f - bb*h
        t10, t11 = a*g - bb*e, a*h - bb*f
        m2 = m - i1*(e*t00 + g*t10)
        n2 = n - i1*(e*t01 + g*t11)
        o2 = o - i1*(f*t01 + h*t11)
        det2 = m2*o2 - n2*n2
        i2 = 1.0/det2
        u00, u01, u10, u11 = i1*t00, i1*t01, i1*t10, i1*t11
        ia, ib, id_ = i1*a, i1*bb, i1*d
        ja, jb, jd = i2*m2, i2*n2, i2*o2
        put(None, j+q, (det1, det2))
        def apply(X, piv):
            r = [jnp.broadcast_to(X[q+t:q+t+1], (8, 128)) for t in range(4)]
            if piv:
                inp = (lane >= l+q) & (lane < l+q+4)
                r = [jnp.where(inp, jnp.where(lane == l+q+t, 1.0, 0.0), r[t]) for t in range(4)]
            y0, y1 = id_*r[0] - ib*r[1], ia*r[1] - ib*r[0]
            z2 = r[2] - (e*y0 + g*y1)
            z3 = r[3] - (f*y0 + h*y1)
            w2 = jd*z2 - jb*z3
            w3 = ja*z3 - jb*z2
            w0 = (y0 - u01*w3) - u00*w2
            w1 = (y1 - u11*w3) - u10*w2
            W = [w0, w1, w2, w3]
            out = []
            for v in range(G//8):
                xv = X[8*v:8*v+8]
                if piv: xv = jnp.where(inp, 0.0, xv)
                cv = [c[q+t][8*v:8*v+8] for t in range(4)]
                nv = (xv - (cv[2]*w2 + cv[3]*w3)) - (cv[0]*w0 + cv[1]*w1)
                if q//8 == v:
                    for t in range(4): nv = jnp.where(sub[:8] == q%8+t, W[t], nv)
                out.append(nv)
            return jnp.concatenate(out, 0) if len(out) > 1 else out[0]
        nc = list(c)
        for t in range(q+4, G): nc[t] = apply(c[t], False)
        D = [apply(D[i], i == pt) for i in range(len(tiles))]
        c = nc
    out = []
    inpG = (lane >= l) & (lane < l+G)
    for ti, X in enumerate(tiles):
        put(ti, j, D[ti])
        vs = [X[:j+G]]
        if j+G < b:
            R = [jnp.broadcast_to(D[ti][t:t+1], (8, 128)) for t in range(G)]
            for v in range(G//8, (b-j)//8):
                xv = X[j+8*v:j+8*v+8]
                if ti == pt: xv = jnp.where(inpG, 0.0, xv)
                acc = [None]*4
                for t in range(G):
                    pr = call[t][8*v:8*v+8]*R[t]
                    k = t % 4
                    acc[k] = pr if acc[k] is None else acc[k] + pr
                vs.append(xv - ((acc[0]+acc[1]) + (acc[2]+acc[3])))
        out.append(jnp.concatenate(vs, 0) if len(vs) > 1 else vs[0])
    return out

def split(x):
    hi = x.astype(B16); return hi, (x - hi.astype(F32)).astype(B16)
def mm3(a, b, dn):
    (ah, al), (bh, bl) = a, b
    dg = lambda u, v: lax.dot_general(u, v, dn, preferred_element_type=F32)
    return dg(ah, bh) + (dg(ah, bl) + dg(al, bh))
NN = (((1,), (0,)), ((), ()))
TN = (((0,), (0,)), ((), ()))
NT = (((1,), (1,)), ((), ()))


def copy_to(src, dst, send, recv, device):
    return pltpu.make_async_remote_copy(
        src_ref=src, dst_ref=dst, send_sem=send, recv_sem=recv, device_id=(device,), device_id_type=MESH
    )


def kernel(n, s_hbm, w_hbm, g_hbm, x_out, ld_out, s_in, w_in, g_in, S, Sx, W, WB, SB, GB, GX, Uo, CG, Rs, F, ZC, RC, E, Eh, El, DT, Y,
           det, ld_acc, zero_ref, sin, sw, rw, sS, rS, sg, rg, sx, rx):
    height = n.bit_length() - 1
    me = lax.axis_index("leaf")
    R, M = g_hbm.shape
    nk = R // B
    H = R // 2
    C = M // NC
    s_parts = [(slice(0, H), slice(0, R)), (slice(H, R), slice(H, R))]
    y_parts = [slice(C * c, C * c + C + (8 if c == NC - 1 else 0)) for c in range(NC)]
    left = [me % (2 << l) == 0 for l in range(height)]
    gives = [(me + 1) % (2 << l) == 0 for l in range(height)]
    rest = me != 0
    count = lambda flags: sum(f.astype(jnp.int32) for f in flags)
    span = 1 + sum(jnp.where(left[l], 1 << l, 0) for l in range(height))
    top = me - span

    loads = [pltpu.make_async_copy(a, b, sin.at[i]) for i, (a, b) in enumerate([(s_hbm, s_in), (w_hbm, w_in), (g_hbm, g_in)])]
    for load in loads:
        load.start()
    barrier = pltpu.get_barrier_semaphore()
    for l in range(height):
        @pl.when(left[l])
        def _():
            pl.semaphore_signal(barrier, inc=1, device_id=(me + (2 << l) - 1,), device_id_type=MESH)
            pl.semaphore_signal(barrier, inc=1, device_id=(me + (1 << l),), device_id_type=MESH)
    @pl.when(rest)
    def _():
        pl.semaphore_signal(barrier, inc=1, device_id=(top,), device_id_type=MESH)

    loads[0].wait()
    s0 = s_in[...]
    eye = iota((R, R), 0) == iota((R, R), 1)
    diag = jnp.where(eye, s0, 0.0)
    drow = jnp.sum(diag, axis=0, keepdims=True)
    scol = lax.rsqrt(jnp.sum(diag, axis=1, keepdims=True))
    srow = lax.rsqrt(drow)
    S[...] = s0 * scol * srow
    loads[1].wait()
    W[...] = w_in[...] * scol
    loads[2].wait()
    CG[:, R:] = g_in[...] * scol
    zero_ref[...] = jnp.zeros_like(zero_ref)
    WB[height] = jnp.zeros((R, R), F32)
    ld_acc[...] = jnp.broadcast_to(jnp.sum(jnp.log(drow), axis=1, keepdims=True), (8, 128))
    pl.semaphore_wait(barrier, count(left) + count(gives) + rest.astype(jnp.int32))

    def send_state(level, target):
        for i, part in enumerate(s_parts):
            Sx[part] = S[part]
            copy_to(Sx.at[part], SB.at[(level,) + part], sS.at[i], rS.at[level, i], target).start()

    def send_rhs(level, target):
        GX[:R, :] = CG[:, R:]
        GX[R:, :] = ld_acc[...]
        copy_to(GX, GB.at[level], sg, rg.at[level], target).start()

    @pl.when(me % 2 != 0)
    def _():
        send_state(0, me - 1)
    for l in range(height):
        @pl.when(gives[l])
        def _():
            copy_to(W, WB.at[l], sw.at[l], rw.at[l], me + 1 - (2 << l)).start()
    @pl.when(me % 2 != 0)
    def _():
        send_rhs(0, me - 1)

    row = iota((B, 128), 0)
    lane = iota((B, 128), 1)

    def level(it, st):
        last = it == height

        @pl.when(me % (2 * st) == 0)
        def _():
            @pl.when(jnp.logical_not(last))
            def _():
                copy_to(W, WB.at[it], sw.at[0], rw.at[it], me).wait_recv()
            zero = zero_ref[...]
            for k in range(nk):
                lb = (B * k) % 128
                base = B * k - lb
                lo = B * (k + 1)
                rows, pair = slice(B * k, lo), slice(base, base + 128)
                tiles = [S[rows, t:t + 128] for t in range(base, R, 128)]
                def put(ti, j, val):
                    if ti is None:
                        r0 = (rows.start + j) // 2
                        det[r0:r0 + 1, :] = val[0][0:1]
                        det[r0 + 1:r0 + 2, :] = val[1][0:1]
                    else:
                        Rs[rows.start + j:rows.start + j + G, base + 128 * ti:base + 128 * ti + 128] = val
                for j in range(0, B, G):
                    tiles = group(tiles, 0, j, lb + j, G, zero, put)
                Z = jnp.concatenate(tiles, 1) if len(tiles) > 1 else tiles[0]
                zs = split(Z)
                if k < nk - 1:
                    upd = mm3(zs, split(Rs[rows, base:]), TN)
                    S[lo:, base:] -= upd[lo - base:]
                if k == 0:
                    wb = WB[it]
                    CG[:, :R] = 0.5 * mm3(split(W[...]), split(wb), NT)
                rel = lane - lb
                inside = (rel >= 0) & (rel < B)
                Lk = jnp.where(inside & (rel < G * (row // G)), tiles[0], jnp.where(rel == row, 1.0, 0.0))
                DLk = jnp.where(inside & (rel < G * (row // G) + G), Rs[rows, pair], 0.0)
                both = mm3(split(jnp.concatenate([Lk, DLk], 0)), split(CG[pair, :]), NN)
                ZC[rows, :] = both[:B, :R]
                rc = both[B:]
                RC[rows, :] = rc
                ls = split(Lk)
                if k < nk - 1:
                    upd = mm3(zs, split(rc), TN)
                    CG[lo:, :] -= upd[lo - base:]
                    rs = Rs[rows, base:]
                    rs = jnp.where(iota(rs.shape, 1) >= lo - base, rs, 0.0)
                    ft = mm3(ls, split(rs), TN)[lb:lb + B]
                    F[rows, base:] = ft
                    ek = mm3(ls, split(rc), TN)[lb:lb + B]
                    E[rows, :] = ek
                    if k:
                        f = jnp.where((iota((B * k, 128), 1) >= lb) & (iota((B * k, 128), 1) < lb + B), F[:B * k, pair], 0.0)
                        gap = jnp.zeros_like
                        pad = (lambda v: jnp.concatenate([v, gap(v)], 0)) if lb == 0 else (lambda v: jnp.concatenate([gap(v), v], 0))
                        fs = split(f)
                        E[:B * k, :] -= mm3(fs, split(pad(ek)), NN)
                        F[:B * k, base:] -= mm3(fs, split(pad(ft)), NN)
                if k == nk - 2:
                    zc, rr = split(ZC[:lo, :]), split(RC[:lo, :])
                    Uo[:H, :] = mm3([a[:, :H] for a in zc], rr, TN)
                    Uo[H:, H:] = mm3([a[:, H:] for a in zc], [a[:, H:] for a in rr], TN)

            ek = mm3(ls, split(rc), TN)[lb:]
            E[rows, :] = ek
            f = jnp.where(iota((R - B, 128), 1) >= lb, F[:R - B, pair], 0.0)
            E[:R - B, :] -= mm3(split(f), split(jnp.concatenate([jnp.zeros_like(ek), ek], 0)), NN)
            et = E[...]
            Eh[it], El[it] = split(et[:, :R].T)
            DT[it] = et[:, R:].T
            ld_acc[...] += jnp.broadcast_to(jnp.sum(jnp.log(det[...]), axis=0, keepdims=True), (8, 128))

            @pl.when(jnp.logical_not(last))
            def _():
                for i, part in enumerate(s_parts):
                    copy_to(Sx.at[part], SB.at[(it,) + part], sS.at[i], rS.at[it, i], me).wait_recv()
                zc, rr = split(ZC[rows, :]), split(RC[rows, :])
                ua = Uo[:H, :] + mm3([a[:, :H] for a in zc], rr, TN)
                ub = Uo[H:, H:] + mm3([a[:, H:] for a in zc], [a[:, H:] for a in rr], TN)
                S[:H, :] = SB[it, :H, :] - ua[:, :R]
                S[H:, H:] = SB[it, H:, H:] - ub[:, :H]
                turn = me % (4 * st) != 0
                @pl.when(turn)
                def _():
                    send_state(it + 1, top)
                copy_to(GX, GB.at[it], sg, rg.at[it], me).wait_recv()
                CG[:H, R:] = GB[it, :H] - ua[:, R:]
                CG[H:, R:] = GB[it, H:R] - ub[:, H:]
                ld_acc[...] += GB[it, R:]
                @pl.when(turn)
                def _():
                    send_rhs(it + 1, top)
                W[...] = WB[it]
        return st * 2

    lax.fori_loop(0, height + 1, level, jnp.int32(1))

    @pl.when(jnp.logical_not(rest))
    def _():
        Y[height, :M, :] = DT[height]
        Y[height, M:, :] = jnp.broadcast_to(ld_acc[0:1, 0:1] / (R * n), (8, R))

    def down(i, st):
        it = height - 1 - i

        @pl.when(me % (2 * st) == 0)
        def _():
            for c in range(NC):
                @pl.when(rest & (span == 2 * st))
                def _():
                    copy_to(Y.at[it + 1, y_parts[c]], Y.at[it + 1, y_parts[c]], sx.at[it, c], rx.at[c], me).wait_recv()
                copy_to(Y.at[it + 1, y_parts[c]], Y.at[it, y_parts[c]], sx.at[it, c], rx.at[c], me + st).start()
            for c in range(NC):
                r = slice(C * c, C * c + C)
                ah, al = split(Y[it + 1, r, :])
                dg = lambda a, b: jnp.dot(a, b, preferred_element_type=F32)
                Y[it, r, :] = DT[it, r, :] - (dg(ah, Eh[it]) + (dg(al, Eh[it]) + dg(ah, El[it])))
            Y[it, M:, :] = Y[it + 1, M:, :]
        return st // 2

    lax.fori_loop(0, height, down, jnp.int32(n // 2))

    @pl.when(me % 2 != 0)
    def _():
        for c in range(NC):
            copy_to(Y.at[0, y_parts[c]], Y.at[0, y_parts[c]], sx.at[0, c], rx.at[c], top).wait_recv()
    x_out[...] = (Y[0, :M, :] * srow).T
    ld_out[...] = Y[0, M:M + 1, 0:1]
    for l in range(height):
        @pl.when(gives[l])
        def _():
            copy_to(W, WB.at[l], sw.at[l], rw.at[l], me + 1 - (2 << l)).wait_send()
        @pl.when(left[l])
        def _():
            for c in range(NC):
                copy_to(Y.at[0, y_parts[c]], Y.at[0, y_parts[c]], sx.at[l, c], rx.at[c], me + (1 << l)).wait_send()
    @pl.when(rest)
    def _():
        for i, part in enumerate(s_parts):
            copy_to(Sx.at[part], SB.at[(0,) + part], sS.at[i], rS.at[0, i], top).wait_send()
        copy_to(GX, GB.at[0], sg, rg.at[0], top).wait_send()


def local(n, blocks, generators, rhs_blocks):
    R, M = rhs_blocks.shape
    height = n.bit_length() - 1
    dma = pltpu.SemaphoreType.DMA
    vm = lambda *s: pltpu.VMEM(s, F32)
    half = pltpu.VMEM((height + 1, R, R), B16)
    x, ld = pl.pallas_call(
        functools.partial(kernel, n),
        out_shape=(jax.ShapeDtypeStruct((R, M), F32), jax.ShapeDtypeStruct((1, 1), F32)),
        in_specs=[pl.BlockSpec(memory_space=pl.ANY)] * 3,
        out_specs=[pl.BlockSpec(memory_space=pltpu.VMEM)] * 2,
        scratch_shapes=[
            vm(R, R), vm(R, R), vm(R, M), vm(R, R), vm(R, R), vm(R, R), vm(height + 1, R, R), vm(height, R, R), vm(height, R + 8, M),
            vm(R + 8, M), vm(R, R + M), vm(R, R + M), vm(R, R), vm(R, R), vm(R, R), vm(R, R + M), vm(R, R + M), half, half,
            vm(height + 1, M, R), vm(height + 1, M + 8, R), vm(R // 2, 128), vm(8, 128), vm(G, 128),
            dma((3,)), dma((height,)), dma((height,)), dma((2,)), dma((height, 2)), dma, dma((height,)), dma((height, NC)), dma((NC,)),
        ],
        compiler_params=pltpu.CompilerParams(
            collective_id=0, has_side_effects=True, vmem_limit_bytes=48 * 1024 * 1024
        ),
        name="ulv",
    )(blocks, generators, rhs_blocks)
    return x, ld.reshape(())


def solution(mesh):
    n = mesh.shape["leaf"]
    return jax.shard_map(
        functools.partial(local, n),
        mesh=mesh,
        in_specs=(P("leaf", None), P("leaf", None), P("leaf", None)),
        out_specs=(P("leaf", None), P()),
        check_vma=False,
    )
```

time: 161 us -> 116 us (0.72)
  the two profiles are of different devices: /device:TPU:1 before, /device:TPU:255 now
where the time goes in v2:
time: 116 us
  Pallas kernels  110 us (95%)
  local copies, waits for them, and re-layouts  3.45 us (3%)
  between operations  2.39 us (2%)
    pallas_call x1, Pallas kernels, local(): pl.pallas_call(functools.partial(kernel, n), out_shape=(jax.ShapeDtypeStr...  110 us
    unnamed x7, local copies, waits for them, and re-layouts  3.45 us

profile of v2, /device:TPU:255, one launch (start us, length us, event | category | flops | bytes accessed | tf_op | source)
XLA Modules:
  0.0 115.6 jit_solution(12041989855305554470)
XLA Ops:
  0.6 0.0 copy-start
  0.6 0.9 copy-done
  1.6 0.0 copy-start.1
  1.6 0.9 copy-done.1
  2.5 0.0 copy-start.2
  2.5 0.9 copy-done.2
  3.4 109.7 %ulv.1 = (f32[256,128]{1,0:T(8,128)S(1)}, f32[1,1]{1,0:T(1,128)}) custom-call(f32[256,256]{1,0:T(8,128)S(1)} %copy-done, f32[256,256]{1,0:T(8,128)S(1)} %copy-done.1, f32[256,128]{1,0:T(8,128)S(1)} %copy-done.2), custom_call_target="tpu_custom_call" | custom-call | tf_op jit(solution)/shard_map/ulv/pallas_call | solution.py:326
  113.2 0.7 copy.7
Async XLA Ops:
  0.6 1.0 copy-start
  1.6 0.9 copy-start.1
  2.5 0.9 copy-start.2

commit v3 on v2

--- a/solution.py
+++ b/solution.py
@@ -41,11 +41,7 @@
         ia, ib, id_ = i1*a, i1*bb, i1*d
         ja, jb, jd = i2*m2, i2*n2, i2*o2
         put(None, j+q, (det1, det2))
-        def apply(X, piv):
-            r = [jnp.broadcast_to(X[q+t:q+t+1], (8, 128)) for t in range(4)]
-            if piv:
-                inp = (lane >= l+q) & (lane < l+q+4)
-                r = [jnp.where(inp, jnp.where(lane == l+q+t, 1.0, 0.0), r[t]) for t in range(4)]
+        def solve(r):
             y0, y1 = id_*r[0] - ib*r[1], ia*r[1] - ib*r[0]
             z2 = r[2] - (e*y0 + g*y1)
             z3 = r[3] - (f*y0 + h*y1)
@@ -53,7 +49,14 @@
             w3 = ja*z3 - jb*z2
             w0 = (y0 - u01*w3) - u00*w2
             w1 = (y1 - u11*w3) - u10*w2
-            W = [w0, w1, w2, w3]
+            return [w0, w1, w2, w3]
+        def apply(X, piv):
+            r = [jnp.broadcast_to(X[q+t:q+t+1], (8, 128)) for t in range(4)]
+            if piv:
+                inp = (lane >= l+q) & (lane < l+q+4)
+                r = [jnp.where(inp, jnp.where(lane == l+q+t, 1.0, 0.0), r[t]) for t in range(4)]
+            W = solve(r)
+            w0, w1, w2, w3 = W
             out = []
             for v in range(G//8):
                 xv = X[8*v:8*v+8]
@@ -65,7 +68,13 @@
                 out.append(nv)
             return jnp.concatenate(out, 0) if len(out) > 1 else out[0]
         nc = list(c)
-        for t in range(q+4, G): nc[t] = apply(c[t], False)
+        if q + 4 < G:
+            W = solve([c[q+t] for t in range(4)])
+            for t in range(q+4, G):
+                w = [jnp.broadcast_to(x[t:t+1], (8, 128)) for x in W]
+                nv = (c[t] - (c[q+2]*w[2] + c[q+3]*w[3])) - (c[q]*w[0] + c[q+1]*w[1])
+                for u in range(4): nv = jnp.where(sub[:8] == q+u, w[u], nv)
+                nc[t] = nv
         D = [apply(D[i], i == pt) for i in range(len(tiles))]
         c = nc
     out = []
@@ -105,7 +114,7 @@
 
 
 def kernel(n, s_hbm, w_hbm, g_hbm, x_out, ld_out, s_in, w_in, g_in, S, Sx, W, WB, SB, GB, GX, Uo, CG, Rs, F, ZC, RC, E, Eh, El, DT, Y,
-           det, ld_acc, zero_ref, sin, sw, rw, sS, rS, sg, rg, sx, rx):
+           det, ld_acc, zero_ref, sin, sw, rw, sS, rS, sg, rg, sx, sx2, rx):
     height = n.bit_length() - 1
     me = lax.axis_index("leaf")
     R, M = g_hbm.shape
@@ -120,6 +129,12 @@
     count = lambda flags: sum(f.astype(jnp.int32) for f in flags)
     span = 1 + sum(jnp.where(left[l], 1 << l, 0) for l in range(height))
     top = me - span
+    upper = [(height - 1 - l) % 2 == 0 for l in range(height)]
+    skips = [(l > 0) and upper[l] for l in range(height)]
+    single = [left[l] if upper[l] else (me % (4 << l) == 0) for l in range(height)]
+    double = [left[l] if skips[l] else (me % 2 > 1) for l in range(height)]
+    far = sum(jnp.where((span == 1 << l) & (me // (2 << l) % 2 == 1), 2 << l, 0) for l in range(height) if not upper[l])
+    source = top - far
 
     loads = [pltpu.make_async_copy(a, b, sin.at[i]) for i, (a, b) in enumerate([(s_hbm, s_in), (w_hbm, w_in), (g_hbm, g_in)])]
     for load in loads:
@@ -132,7 +147,7 @@
             pl.semaphore_signal(barrier, inc=1, device_id=(me + (1 << l),), device_id_type=MESH)
     @pl.when(rest)
     def _():
-        pl.semaphore_signal(barrier, inc=1, device_id=(top,), device_id_type=MESH)
+        pl.semaphore_signal(barrier, inc=1, device_id=(source,), device_id_type=MESH)
 
     loads[0].wait()
     s0 = s_in[...]
@@ -149,7 +164,7 @@
     zero_ref[...] = jnp.zeros_like(zero_ref)
     WB[height] = jnp.zeros((R, R), F32)
     ld_acc[...] = jnp.broadcast_to(jnp.sum(jnp.log(drow), axis=1, keepdims=True), (8, 128))
-    pl.semaphore_wait(barrier, count(left) + count(gives) + rest.astype(jnp.int32))
+    pl.semaphore_wait(barrier, count(single) + count(double) + count(gives) + rest.astype(jnp.int32))
 
     def send_state(level, target):
         for i, part in enumerate(s_parts):
@@ -281,11 +296,18 @@
 
         @pl.when(me % (2 * st) == 0)
         def _():
+            high = i % 2 == 0
             for c in range(NC):
+                part = Y.at[it + 1, y_parts[c]]
                 @pl.when(rest & (span == 2 * st))
                 def _():
-                    copy_to(Y.at[it + 1, y_parts[c]], Y.at[it + 1, y_parts[c]], sx.at[it, c], rx.at[c], me).wait_recv()
-                copy_to(Y.at[it + 1, y_parts[c]], Y.at[it, y_parts[c]], sx.at[it, c], rx.at[c], me + st).start()
+                    copy_to(part, part, sx.at[it, c], rx.at[c], me).wait_recv()
+                @pl.when(high | (me % (4 * st) == 0))
+                def _():
+                    copy_to(part, Y.at[it, y_parts[c]], sx.at[it, c], rx.at[c], me + st).start()
+                @pl.when(high & (it > 0))
+                def _():
+                    copy_to(part, Y.at[it - 1, y_parts[c]], sx2.at[it, c], rx.at[c], me + st + st // 2).start()
             for c in range(NC):
                 r = slice(C * c, C * c + C)
                 ah, al = split(Y[it + 1, r, :])
@@ -299,17 +321,21 @@
     @pl.when(me % 2 != 0)
     def _():
         for c in range(NC):
-            copy_to(Y.at[0, y_parts[c]], Y.at[0, y_parts[c]], sx.at[0, c], rx.at[c], top).wait_recv()
+            copy_to(Y.at[0, y_parts[c]], Y.at[0, y_parts[c]], sx.at[0, c], rx.at[c], source).wait_recv()
     x_out[...] = (Y[0, :M, :] * srow).T
     ld_out[...] = Y[0, M:M + 1, 0:1]
     for l in range(height):
         @pl.when(gives[l])
         def _():
             copy_to(W, WB.at[l], sw.at[l], rw.at[l], me + 1 - (2 << l)).wait_send()
-        @pl.when(left[l])
+        @pl.when(single[l])
         def _():
             for c in range(NC):
                 copy_to(Y.at[0, y_parts[c]], Y.at[0, y_parts[c]], sx.at[l, c], rx.at[c], me + (1 << l)).wait_send()
+        @pl.when(double[l])
+        def _():
+            for c in range(NC):
+                copy_to(Y.at[0, y_parts[c]], Y.at[0, y_parts[c]], sx2.at[l, c], rx.at[c], me + (1 << l)).wait_send()
     @pl.when(rest)
     def _():
         for i, part in enumerate(s_parts):
@@ -332,10 +358,10 @@
             vm(R, R), vm(R, R), vm(R, M), vm(R, R), vm(R, R), vm(R, R), vm(height + 1, R, R), vm(height, R, R), vm(height, R + 8, M),
             vm(R + 8, M), vm(R, R + M), vm(R, R + M), vm(R, R), vm(R, R), vm(R, R), vm(R, R + M), vm(R, R + M), half, half,
             vm(height + 1, M, R), vm(height + 1, M + 8, R), vm(R // 2, 128), vm(8, 128), vm(G, 128),
-            dma((3,)), dma((height,)), dma((height,)), dma((2,)), dma((height, 2)), dma, dma((height,)), dma((height, NC)), dma((NC,)),
+            dma((3,)), dma((height,)), dma((height,)), dma((2,)), dma((height, 2)), dma, dma((height,)), dma((height, NC)), dma((height, NC)), dma((NC,)),
         ],
         compiler_params=pltpu.CompilerParams(
-            collective_id=0, has_side_effects=True, vmem_limit_bytes=48 * 1024 * 1024
+            collective_id=0, has_side_effects=True, vmem_limit_bytes=60 * 1024 * 1024
         ),
         name="ulv",
     )(blocks, generators, rhs_blocks)

time: 116 us -> 107 us (0.922)
  the two profiles are of different devices: /device:TPU:255 before, /device:TPU:103 now
where the time goes in v3:
time: 107 us; the launch traced here: 106 us
  Pallas kernels  102 us (95%)
  between operations  2.45 us (2%)
  local copies, waits for them, and re-layouts  1.57 us (1%)
    pallas_call x1, Pallas kernels, local(): pl.pallas_call(functools.partial(kernel, n), out_shape=(jax.ShapeDtypeStr...  102 us

profile of v3, /device:TPU:103, one launch (start us, length us, event | category | flops | bytes accessed | tf_op | source)
XLA Modules:
  0.0 106.4 jit_solution(13779938660208101579)
XLA Ops:
  0.6 102.4 %ulv.1 = (f32[256,128]{1,0:T(8,128)}, f32[1,1]{1,0:T(1,128)}) custom-call(f32[256,256]{1,0:T(8,128)} %s_hbm.1, f32[256,256]{1,0:T(8,128)} %w_hbm.1, f32[256,128]{1,0:T(8,128)} %g_hbm.1), custom_call_target="tpu_custom_call" | custom-call | tf_op jit(solution)/shard_map/ulv/pallas_call | solution.py:352
  103.0 1.6 %copy.7 = f32[256,128]{1,0:T(8,128)} copy(f32[256,128]{1,0:T(8,128)} %get-tuple-element.8) | data formatting | bytes 262144

commit v4 on v3

--- a/solution.py
+++ b/solution.py
@@ -16,13 +16,29 @@
 
 def iota(shape, dim): return lax.broadcasted_iota(jnp.int32, shape, dim)
 
-def group(tiles, pt, j, l, G, zero, put):
+def sweep(tiles, pt, l, G, zero, put):
+    b = tiles[0].shape[0]
+    spread = lambda r, c0: [jnp.broadcast_to(tiles[pt][r:r + G, c0+t:c0+t+1], (G, 128)) for t in range(G)]
+    c = None
+    for j in range(0, b, G):
+        if c is None:
+            c = [x + zero for x in spread(j, l + j)]
+        ahead = later = None
+        if j + G < b:
+            ahead, later = spread(j + G, l + j), spread(j + G, l + j + G)
+        tiles, c = half(tiles, pt, j, l + j, G, c, ahead, later, zero, put)
+    return tiles
+
+
+def half(tiles, pt, j, l, G, c, ahead, later, zero, put):
     b = tiles[0].shape[0]
     T = tiles[pt]
-    call = [jnp.broadcast_to(T[j:, l+t:l+t+1], (b-j, 128)) for t in range(G)]
-    c = [x[:G] + zero for x in call]
     D = [X[j:j+G] for X in tiles]
+    low = [jnp.broadcast_to(T[j+G:, l+t:l+t+1], (b-j-G, 128)) for t in range(G)] if j+G < b else None
     lane = iota((8, 128), 1); sub = iota((G, 128), 0)
+    if ahead is not None:
+        A = [x + zero for x in ahead]
+        V = list(A)
     for q in range(0, G, 4):
         p = lambda s, t: jnp.broadcast_to(c[q+t][q+s:q+s+1], (8, 128))
         a, bb, d = p(0,0), p(0,1), p(1,1)
@@ -41,6 +57,7 @@
         ia, ib, id_ = i1*a, i1*bb, i1*d
         ja, jb, jd = i2*m2, i2*n2, i2*o2
         put(None, j+q, (det1, det2))
+        cs = lambda u, t, c=c: jnp.broadcast_to(c[t][u:u+1], (8, 128))
         def solve(r):
             y0, y1 = id_*r[0] - ib*r[1], ia*r[1] - ib*r[0]
             z2 = r[2] - (e*y0 + g*y1)
@@ -75,9 +92,24 @@
                 nv = (c[t] - (c[q+2]*w[2] + c[q+3]*w[3])) - (c[q]*w[0] + c[q+1]*w[1])
                 for u in range(4): nv = jnp.where(sub[:8] == q+u, w[u], nv)
                 nc[t] = nv
+        if ahead is not None:
+            W = solve(V[q:q+4])
+            for u in range(G):
+                if not q <= u < q + 4:
+                    V[u] = (V[u] - (cs(u, q+2)*W[2] + cs(u, q+3)*W[3])) - (cs(u, q)*W[0] + cs(u, q+1)*W[1])
+            V[q:q+4] = W
         D = [apply(D[i], i == pt) for i in range(len(tiles))]
         c = nc
     out = []
+    if ahead is not None:
+        fresh = []
+        for t in range(G):
+            acc = [None]*4
+            for u in range(G):
+                pr = A[u]*jnp.broadcast_to(V[u][t:t+1], (8, 128))
+                acc[u % 4] = pr if acc[u % 4] is None else acc[u % 4] + pr
+            fresh.append((later[t] + zero) - ((acc[0]+acc[1]) + (acc[2]+acc[3])))
+        later = fresh
     inpG = (lane >= l) & (lane < l+G)
     for ti, X in enumerate(tiles):
         put(ti, j, D[ti])
@@ -89,12 +121,12 @@
                 if ti == pt: xv = jnp.where(inpG, 0.0, xv)
                 acc = [None]*4
                 for t in range(G):
-                    pr = call[t][8*v:8*v+8]*R[t]
+                    pr = low[t][8*(v-G//8):8*(v-G//8)+8]*R[t]
                     k = t % 4
                     acc[k] = pr if acc[k] is None else acc[k] + pr
                 vs.append(xv - ((acc[0]+acc[1]) + (acc[2]+acc[3])))
         out.append(jnp.concatenate(vs, 0) if len(vs) > 1 else vs[0])
-    return out
+    return out, later
 
 def split(x):
     hi = x.astype(B16); return hi, (x - hi.astype(F32)).astype(B16)
@@ -198,23 +230,25 @@
             @pl.when(jnp.logical_not(last))
             def _():
                 copy_to(W, WB.at[it], sw.at[0], rw.at[it], me).wait_recv()
-            zero = zero_ref[...]
             for k in range(nk):
                 lb = (B * k) % 128
                 base = B * k - lb
                 lo = B * (k + 1)
                 rows, pair = slice(B * k, lo), slice(base, base + 128)
-                tiles = [S[rows, t:t + 128] for t in range(base, R, 128)]
-                def put(ti, j, val):
-                    if ti is None:
-                        r0 = (rows.start + j) // 2
-                        det[r0:r0 + 1, :] = val[0][0:1]
-                        det[r0 + 1:r0 + 2, :] = val[1][0:1]
-                    else:
-                        Rs[rows.start + j:rows.start + j + G, base + 128 * ti:base + 128 * ti + 128] = val
-                for j in range(0, B, G):
-                    tiles = group(tiles, 0, j, lb + j, G, zero, put)
-                Z = jnp.concatenate(tiles, 1) if len(tiles) > 1 else tiles[0]
+                def eliminate():
+                    tiles = [S[rows, t:t + 128] for t in range(base, R, 128)]
+                    def put(ti, j, val):
+                        if ti is None:
+                            r0 = (rows.start + j) // 2
+                            det[r0:r0 + 1, :] = val[0][0:1]
+                            det[r0 + 1:r0 + 2, :] = val[1][0:1]
+                        else:
+                            Rs[rows.start + j:rows.start + j + G, base + 128 * ti:base + 128 * ti + 128] = val
+                    tiles = sweep(tiles, 0, lb, G, zero_ref[...], put)
+                    for i, t in enumerate(tiles):
+                        S[rows, base + 128 * i:base + 128 * i + 128] = t
+                eliminate()
+                Z = S[rows, base:]
                 zs = split(Z)
                 if k < nk - 1:
                     upd = mm3(zs, split(Rs[rows, base:]), TN)
@@ -224,7 +258,7 @@
                     CG[:, :R] = 0.5 * mm3(split(W[...]), split(wb), NT)
                 rel = lane - lb
                 inside = (rel >= 0) & (rel < B)
-                Lk = jnp.where(inside & (rel < G * (row // G)), tiles[0], jnp.where(rel == row, 1.0, 0.0))
+                Lk = jnp.where(inside & (rel < G * (row // G)), Z[:, :128], jnp.where(rel == row, 1.0, 0.0))
                 DLk = jnp.where(inside & (rel < G * (row // G) + G), Rs[rows, pair], 0.0)
                 both = mm3(split(jnp.concatenate([Lk, DLk], 0)), split(CG[pair, :]), NN)
                 ZC[rows, :] = both[:B, :R]

time: 107 us -> 94 us (0.88)
  Pallas kernels: 102 us -> 89.9 us
    pallas_call x1, Pallas kernels: 102 us -> 89.9 us  [local(): pl.pallas_call(functools.partial(kernel, n), out_shape=(jax.ShapeDtypeStr...]
where the time goes in v4:
time: 94 us; the launch traced here: 93.9 us
  Pallas kernels  89.9 us (96%)
  between operations  2.45 us (3%)
  local copies, waits for them, and re-layouts  1.57 us (2%)
    pallas_call x1, Pallas kernels, local(): pl.pallas_call(functools.partial(kernel, n), out_shape=(jax.ShapeDtypeStr...  89.9 us

profile of v4, /device:TPU:103, one launch (start us, length us, event | category | flops | bytes accessed | tf_op | source)
XLA Modules:
  0.0 93.9 jit_solution(14419067733538719984)
XLA Ops:
  0.6 89.9 %ulv.1 = (f32[256,128]{1,0:T(8,128)}, f32[1,1]{1,0:T(1,128)}) custom-call(f32[256,256]{1,0:T(8,128)} %s_hbm.1, f32[256,256]{1,0:T(8,128)} %w_hbm.1, f32[256,128]{1,0:T(8,128)} %g_hbm.1), custom_call_target="tpu_custom_call" | custom-call | tf_op jit(solution)/shard_map/ulv/pallas_call | solution.py:386
  90.5 1.6 %copy.7 = f32[256,128]{1,0:T(8,128)} copy(f32[256,128]{1,0:T(8,128)} %get-tuple-element.8) | data formatting | bytes 262144

commit v5 on v4

--- a/solution.py
+++ b/solution.py
@@ -145,7 +145,7 @@
     )
 
 
-def kernel(n, s_hbm, w_hbm, g_hbm, x_out, ld_out, s_in, w_in, g_in, S, Sx, W, WB, SB, GB, GX, Uo, CG, Rs, F, ZC, RC, E, Eh, El, DT, Y,
+def kernel(n, s_hbm, w_hbm, g_hbm, x_out, ld_out, s_in, w_in, g_in, S, Sx, W, WB, SB, GB, GX, Uo, CG, Rs, F, ZC, RC, L3, E, Eh, El, DT, Y,
            det, ld_acc, zero_ref, sin, sw, rw, sS, rS, sg, rg, sx, sx2, rx):
     height = n.bit_length() - 1
     me = lax.axis_index("leaf")
@@ -195,6 +195,8 @@
     CG[:, R:] = g_in[...] * scol
     zero_ref[...] = jnp.zeros_like(zero_ref)
     WB[height] = jnp.zeros((R, R), F32)
+    for ref in (F, E, RC, L3):
+        ref[...] = jnp.zeros_like(ref)
     ld_acc[...] = jnp.broadcast_to(jnp.sum(jnp.log(drow), axis=1, keepdims=True), (8, 128))
     pl.semaphore_wait(barrier, count(single) + count(double) + count(gives) + rest.astype(jnp.int32))
 
@@ -222,6 +224,15 @@
     row = iota((B, 128), 0)
     lane = iota((B, 128), 1)
 
+    def finish(slot):
+        lb = (R - B) % 128
+        ek = mm3(split(L3[...]), split(RC[R - B:, :]), TN)[lb:]
+        f = F[:R - B, R - 128:]
+        f = jnp.where(iota(f.shape, 1) >= lb, f, 0.0)
+        et = jnp.concatenate([E[:R - B, :] - mm3(split(f), split(jnp.concatenate([jnp.zeros_like(ek), ek], 0)), NN), ek], 0)
+        Eh[slot], El[slot] = split(et[:, :R].T)
+        DT[slot] = et[:, R:].T
+
     def level(it, st):
         last = it == height
 
@@ -230,6 +241,7 @@
             @pl.when(jnp.logical_not(last))
             def _():
                 copy_to(W, WB.at[it], sw.at[0], rw.at[it], me).wait_recv()
+            finish(it)
             for k in range(nk):
                 lb = (B * k) % 128
                 base = B * k - lb
@@ -286,31 +298,25 @@
                     Uo[:H, :] = mm3([a[:, :H] for a in zc], rr, TN)
                     Uo[H:, H:] = mm3([a[:, H:] for a in zc], [a[:, H:] for a in rr], TN)
 
-            ek = mm3(ls, split(rc), TN)[lb:]
-            E[rows, :] = ek
-            f = jnp.where(iota((R - B, 128), 1) >= lb, F[:R - B, pair], 0.0)
-            E[:R - B, :] -= mm3(split(f), split(jnp.concatenate([jnp.zeros_like(ek), ek], 0)), NN)
-            et = E[...]
-            Eh[it], El[it] = split(et[:, :R].T)
-            DT[it] = et[:, R:].T
+            L3[...] = Lk
+            zc, rr = split(ZC[rows, :]), split(rc)
+            Uo[:H, :] += mm3([a[:, :H] for a in zc], rr, TN)
+            Uo[H:, H:] += mm3([a[:, H:] for a in zc], [a[:, H:] for a in rr], TN)
             ld_acc[...] += jnp.broadcast_to(jnp.sum(jnp.log(det[...]), axis=0, keepdims=True), (8, 128))
 
             @pl.when(jnp.logical_not(last))
             def _():
                 for i, part in enumerate(s_parts):
                     copy_to(Sx.at[part], SB.at[(it,) + part], sS.at[i], rS.at[it, i], me).wait_recv()
-                zc, rr = split(ZC[rows, :]), split(RC[rows, :])
-                ua = Uo[:H, :] + mm3([a[:, :H] for a in zc], rr, TN)
-                ub = Uo[H:, H:] + mm3([a[:, H:] for a in zc], [a[:, H:] for a in rr], TN)
-                S[:H, :] = SB[it, :H, :] - ua[:, :R]
-                S[H:, H:] = SB[it, H:, H:] - ub[:, :H]
+                S[:H, :] = SB[it, :H, :] - Uo[:H, :R]
+                S[H:, H:] = SB[it, H:, H:] - Uo[H:, H:R]
                 turn = me % (4 * st) != 0
                 @pl.when(turn)
                 def _():
                     send_state(it + 1, top)
                 copy_to(GX, GB.at[it], sg, rg.at[it], me).wait_recv()
-                CG[:H, R:] = GB[it, :H] - ua[:, R:]
-                CG[H:, R:] = GB[it, H:R] - ub[:, H:]
+                CG[:H, R:] = GB[it, :H] - Uo[:H, R:]
+                CG[H:, R:] = GB[it, H:R] - Uo[H:, R:]
                 ld_acc[...] += GB[it, R:]
                 @pl.when(turn)
                 def _():
@@ -320,9 +326,13 @@
 
     lax.fori_loop(0, height + 1, level, jnp.int32(1))
 
+    @pl.when(me % 2 == 0)
+    def _():
+        finish(count(left) + 1 - rest.astype(jnp.int32))
+
     @pl.when(jnp.logical_not(rest))
     def _():
-        Y[height, :M, :] = DT[height]
+        Y[height, :M, :] = DT[height + 1]
         Y[height, M:, :] = jnp.broadcast_to(ld_acc[0:1, 0:1] / (R * n), (8, R))
 
     def down(i, st):
@@ -346,7 +356,7 @@
                 r = slice(C * c, C * c + C)
                 ah, al = split(Y[it + 1, r, :])
                 dg = lambda a, b: jnp.dot(a, b, preferred_element_type=F32)
-                Y[it, r, :] = DT[it, r, :] - (dg(ah, Eh[it]) + (dg(al, Eh[it]) + dg(ah, El[it])))
+                Y[it, r, :] = DT[it + 1, r, :] - (dg(ah, Eh[it + 1]) + (dg(al, Eh[it + 1]) + dg(ah, El[it + 1])))
             Y[it, M:, :] = Y[it + 1, M:, :]
         return st // 2
 
@@ -382,7 +392,7 @@
     height = n.bit_length() - 1
     dma = pltpu.SemaphoreType.DMA
     vm = lambda *s: pltpu.VMEM(s, F32)
-    half = pltpu.VMEM((height + 1, R, R), B16)
+    half = pltpu.VMEM((height + 2, R, R), B16)
     x, ld = pl.pallas_call(
         functools.partial(kernel, n),
         out_shape=(jax.ShapeDtypeStruct((R, M), F32), jax.ShapeDtypeStruct((1, 1), F32)),
@@ -390,8 +400,8 @@
         out_specs=[pl.BlockSpec(memory_space=pltpu.VMEM)] * 2,
         scratch_shapes=[
             vm(R, R), vm(R, R), vm(R, M), vm(R, R), vm(R, R), vm(R, R), vm(height + 1, R, R), vm(height, R, R), vm(height, R + 8, M),
-            vm(R + 8, M), vm(R, R + M), vm(R, R + M), vm(R, R), vm(R, R), vm(R, R), vm(R, R + M), vm(R, R + M), half, half,
-            vm(height + 1, M, R), vm(height + 1, M + 8, R), vm(R // 2, 128), vm(8, 128), vm(G, 128),
+            vm(R + 8, M), vm(R, R + M), vm(R, R + M), vm(R, R), vm(R, R), vm(R, R), vm(R, R + M), vm(B, 128), vm(R, R + M), half, half,
+            vm(height + 2, M, R), vm(height + 1, M + 8, R), vm(R // 2, 128), vm(8, 128), vm(G, 128),
             dma((3,)), dma((height,)), dma((height,)), dma((2,)), dma((height, 2)), dma, dma((height,)), dma((height, NC)), dma((height, NC)), dma((NC,)),
         ],
         compiler_params=pltpu.CompilerParams(

time: 94 us -> 92.6 us (0.985)
  Pallas kernels: 89.9 us -> 88.4 us
    pallas_call x1, Pallas kernels: 89.9 us -> 88.4 us  [local(): pl.pallas_call(functools.partial(kernel, n), out_shape=(jax.ShapeDtypeStr...]
where the time goes in v5:
time: 92.6 us; the launch traced here: 92.5 us
  Pallas kernels  88.4 us (95%)
  between operations  2.45 us (3%)
  local copies, waits for them, and re-layouts  1.57 us (2%)
    pallas_call x1, Pallas kernels, local(): pl.pallas_call(functools.partial(kernel, n), out_shape=(jax.ShapeDtypeStr...  88.4 us

profile of v5, /device:TPU:103, one launch (start us, length us, event | category | flops | bytes accessed | tf_op | source)
XLA Modules:
  0.0 92.5 jit_solution(12241505032201733768)
XLA Ops:
  0.6 88.4 %ulv.1 = (f32[256,128]{1,0:T(8,128)}, f32[1,1]{1,0:T(1,128)}) custom-call(f32[256,256]{1,0:T(8,128)} %s_hbm.1, f32[256,256]{1,0:T(8,128)} %w_hbm.1, f32[256,128]{1,0:T(8,128)} %g_hbm.1), custom_call_target="tpu_custom_call" | custom-call | tf_op jit(solution)/shard_map/ulv/pallas_call | solution.py:396
  89.1 1.6 %copy.7 = f32[256,128]{1,0:T(8,128)} copy(f32[256,128]{1,0:T(8,128)} %get-tuple-element.8) | data formatting | bytes 262144

commit v6 on v5

--- a/solution.py
+++ b/solution.py
@@ -153,7 +153,7 @@
     nk = R // B
     H = R // 2
     C = M // NC
-    s_parts = [(slice(0, H), slice(0, R)), (slice(H, R), slice(H, R))]
+    s_parts = [(slice(0, B), slice(0, R)), (slice(B, H), slice(0, R)), (slice(H, R), slice(H, R))]
     y_parts = [slice(C * c, C * c + C + (8 if c == NC - 1 else 0)) for c in range(NC)]
     left = [me % (2 << l) == 0 for l in range(height)]
     gives = [(me + 1) % (2 << l) == 0 for l in range(height)]
@@ -232,6 +232,18 @@
         et = jnp.concatenate([E[:R - B, :] - mm3(split(f), split(jnp.concatenate([jnp.zeros_like(ek), ek], 0)), NN), ek], 0)
         Eh[slot], El[slot] = split(et[:, :R].T)
         DT[slot] = et[:, R:].T
+
+    def take(l, i):
+        part = s_parts[i]
+        copy_to(Sx.at[part], SB.at[(l,) + part], sS.at[i], rS.at[l, i], me).wait_recv()
+        S[part] = SB[(l,) + part] - Uo[part]
+
+    def take_rest(l):
+        take(l, 1)
+        take(l, 2)
+        copy_to(GX, GB.at[l], sg, rg.at[l], me).wait_recv()
+        CG[:, R:] = GB[l, :R] - Uo[:, R:]
+        ld_acc[...] += GB[l, R:]
 
     def level(it, st):
         last = it == height
@@ -261,13 +273,16 @@
                         S[rows, base + 128 * i:base + 128 * i + 128] = t
                 eliminate()
                 Z = S[rows, base:]
+                if k == 0:
+                    wb = WB[it]
+                    CG[:, :R] = 0.5 * mm3(split(W[...]), split(wb), NT)
+                    @pl.when(it > 0)
+                    def _():
+                        take_rest(it - 1)
                 zs = split(Z)
                 if k < nk - 1:
                     upd = mm3(zs, split(Rs[rows, base:]), TN)
                     S[lo:, base:] -= upd[lo - base:]
-                if k == 0:
-                    wb = WB[it]
-                    CG[:, :R] = 0.5 * mm3(split(W[...]), split(wb), NT)
                 rel = lane - lb
                 inside = (rel >= 0) & (rel < B)
                 Lk = jnp.where(inside & (rel < G * (row // G)), Z[:, :128], jnp.where(rel == row, 1.0, 0.0))
@@ -306,20 +321,11 @@
 
             @pl.when(jnp.logical_not(last))
             def _():
-                for i, part in enumerate(s_parts):
-                    copy_to(Sx.at[part], SB.at[(it,) + part], sS.at[i], rS.at[it, i], me).wait_recv()
-                S[:H, :] = SB[it, :H, :] - Uo[:H, :R]
-                S[H:, H:] = SB[it, H:, H:] - Uo[H:, H:R]
-                turn = me % (4 * st) != 0
-                @pl.when(turn)
+                take(it, 0)
+                @pl.when(me % (4 * st) != 0)
                 def _():
+                    take_rest(it)
                     send_state(it + 1, top)
-                copy_to(GX, GB.at[it], sg, rg.at[it], me).wait_recv()
-                CG[:H, R:] = GB[it, :H] - Uo[:H, R:]
-                CG[H:, R:] = GB[it, H:R] - Uo[H:, R:]
-                ld_acc[...] += GB[it, R:]
-                @pl.when(turn)
-                def _():
                     send_rhs(it + 1, top)
                 W[...] = WB[it]
         return st * 2
@@ -402,7 +408,7 @@
             vm(R, R), vm(R, R), vm(R, M), vm(R, R), vm(R, R), vm(R, R), vm(height + 1, R, R), vm(height, R, R), vm(height, R + 8, M),
             vm(R + 8, M), vm(R, R + M), vm(R, R + M), vm(R, R), vm(R, R), vm(R, R), vm(R, R + M), vm(B, 128), vm(R, R + M), half, half,
             vm(height + 2, M, R), vm(height + 1, M + 8, R), vm(R // 2, 128), vm(8, 128), vm(G, 128),
-            dma((3,)), dma((height,)), dma((height,)), dma((2,)), dma((height, 2)), dma, dma((height,)), dma((height, NC)), dma((height, NC)), dma((NC,)),
+            dma((3,)), dma((height,)), dma((height,)), dma((3,)), dma((height, 3)), dma, dma((height,)), dma((height, NC)), dma((height, NC)), dma((NC,)),
         ],
         compiler_params=pltpu.CompilerParams(
             collective_id=0, has_side_effects=True, vmem_limit_bytes=60 * 1024 * 1024

time: 92.6 us -> 92.5 us (level)
  no operation moved by 1% of the time
where the time goes in v6:
time: 92.5 us; the launch traced here: 92.4 us
  Pallas kernels  88.4 us (96%)
  between operations  2.45 us (3%)
  local copies, waits for them, and re-layouts  1.57 us (2%)
    pallas_call x1, Pallas kernels, local(): pl.pallas_call(functools.partial(kernel, n), out_shape=(jax.ShapeDtypeStr...  88.4 us

profile of v6, /device:TPU:103, one launch (start us, length us, event | category | flops | bytes accessed | tf_op | source)
XLA Modules:
  0.0 92.4 jit_solution(8780798011514880811)
XLA Ops:
  0.6 88.4 %ulv.1 = (f32[256,128]{1,0:T(8,128)}, f32[1,1]{1,0:T(1,128)}) custom-call(f32[256,256]{1,0:T(8,128)} %s_hbm.1, f32[256,256]{1,0:T(8,128)} %w_hbm.1, f32[256,128]{1,0:T(8,128)} %g_hbm.1), custom_call_target="tpu_custom_call" | custom-call | tf_op jit(solution)/shard_map/ulv/pallas_call | solution.py:402
  89.0 1.6 %copy.7 = f32[256,128]{1,0:T(8,128)} copy(f32[256,128]{1,0:T(8,128)} %get-tuple-element.8) | data formatting | bytes 262144
